TPU v7x, 32 devices: a whole 2x2x4 slice. The times are simulated.
32 devices in a mesh: parts: 2 (over y), pair: 16 (over z, x, core).
Axes of the slice: x: 2, y: 2, z: 4, core: 2. Of those that a mesh axis runs over, the one named last changes fastest.
Arguments:
- amplitudes: bfloat16 [32, 8192], P(('parts', 'pair')), parts along dimension 0, may hold values from -6 to 6
- tile_counts: int32 [32], P('parts'), parts along dimension 0, may hold values from 1 to 8, 64 in all
- screen: int32 [256, 16], P(('parts', 'pair')), parts along dimension 0, may hold values from 0 to 23
- ladder_ints: bfloat16 [256, 16, 128, 128], P(('parts', 'pair')), parts along dimension 0, may hold values from -0.125 to 0.125
- hole_ints: bfloat16 [32, 16], P(('parts', 'pair')), parts along dimension 0, may hold values from -1.5 to 1.5
- direct: bfloat16 [32, 8192], P(('parts', 'pair')), parts along dimension 0, may hold values from -6 to 6
- occ_energy: float32 [32], P(('parts', 'pair')), parts along dimension 0, may hold values from -3 to -0.5
- virt_energy: float32 [16384], P('parts'), parts along dimension 0, may hold values from 0.5 to 4
Outputs:
- updated: float32 [32, 8192], P(('parts', 'pair')), parts along dimension 0
There are 2 independent parts, one for each index of `parts`. A program takes and returns all parts, laid end to end along the dimension named above; each array names one. Nothing has to cross between parts.
Inputs may be any that keep to these rules, and one draw needn't show every extreme that they name: `tile_counts`: owner counts sum to 64, and the largest is 8. `screen`: an entry names an extended slot of the owner of its row's tile; it may name an empty slot.
All inputs are finite; a program needn't handle non-finite values.
Results may differ from a plain program's by a relative error of at most 0.0045.
Values may be sent and summed in bfloat16 or wider, within the bound.
A program may use at most 64 MiB of HBM per device.

v0:
```python
import jax
import jax.numpy as jnp
from jax import lax
from jax.sharding import PartitionSpec as P

TILE = 128
CAP = 8


def extended_2(block, sides, width):
    for axis, dim in sides:
        count = lax.axis_size(axis)
        forward = [(i, i + 1) for i in range(count - 1)]
        forward.append((count - 1, 0))
        backward = [(target, source) for source, target in forward]
        low = lax.ppermute(
            lax.slice_in_dim(block, block.shape[dim] - width, None, axis=dim), axis, forward
        )
        high = lax.ppermute(lax.slice_in_dim(block, 0, width, axis=dim), axis, backward)
        block = jnp.concatenate([low, block, high], axis=dim)
    return block


def hole_product(hole_ints, operand):
    return jnp.einsum(
        "ik,ksv->siv",
        lax.all_gather(hole_ints, "pair", axis=0, tiled=True),
        operand,
        preferred_element_type=jnp.float32,
    )


def shards(
    amplitudes, tile_counts, screen, ladder_ints, hole_ints, direct, occ_energy, virt_energy
):
    rows_dev = amplitudes.shape[0]
    pair_count = lax.axis_size("pair")
    tiles_all = amplitudes.shape[1] // TILE
    total_rows = rows_dev * pair_count
    coupling = screen.shape[1]
    offsets = jnp.cumsum(tile_counts) - tile_counts
    slot_range = jnp.arange(CAP, dtype=jnp.int32)
    owner_tiles = offsets[:, None] + slot_range[None, :]
    live_slots = slot_range[None, :] < tile_counts[:, None]
    clipped = jnp.minimum(owner_tiles, tiles_all - 1).reshape(-1)
    by_tile = amplitudes.reshape(rows_dev, tiles_all, TILE)
    outgoing = jnp.take(by_tile, clipped, axis=1)
    outgoing = jnp.where(live_slots.reshape(1, -1, 1), outgoing, jnp.zeros_like(outgoing))
    outgoing = outgoing.reshape(rows_dev, pair_count, CAP, TILE)
    owned = lax.all_to_all(outgoing, "pair", split_axis=1, concat_axis=0, tiled=True).reshape(
        total_rows, CAP, TILE
    )
    extended = extended_2(owned, (("pair", 1),), CAP)

    def ladder_slot(operands):
        chosen, blocks = operands
        picked = jnp.take(extended, chosen, axis=1).reshape(total_rows, coupling * TILE)
        return jnp.dot(
            picked, blocks.reshape(coupling * TILE, TILE), preferred_element_type=jnp.float32
        )

    ladder = lax.map(ladder_slot, (screen, ladder_ints))
    positions = jnp.arange(tiles_all, dtype=jnp.int32)
    owner_of = jnp.sum((offsets[None, :] <= positions[:, None]).astype(jnp.int32), axis=1) - 1
    slot_of = positions - offsets[owner_of]
    source_index = slot_of * pair_count + owner_of

    def to_tiles(received):
        flat = received.reshape(CAP * pair_count, rows_dev, TILE)
        return jnp.take(flat, source_index, axis=0)

    hole = hole_product(hole_ints, owned)
    ladder_home, hole_home = (
        lax.all_to_all(
            ladder.reshape(CAP, pair_count, rows_dev, TILE),
            "pair",
            split_axis=1,
            concat_axis=1,
            tiled=True,
        ),
        lax.all_to_all(
            hole.reshape(CAP, pair_count, rows_dev, TILE),
            "pair",
            split_axis=1,
            concat_axis=1,
            tiled=True,
        ),
    )
    coupled = (to_tiles(ladder_home) + to_tiles(hole_home)).astype(jnp.bfloat16)
    summed = jnp.transpose(coupled.astype(jnp.float32), (1, 0, 2)).reshape(
        rows_dev, tiles_all * TILE
    )
    summed = summed + direct.astype(jnp.float32)
    denominator = virt_energy[None, :] - occ_energy[:, None]
    return summed / denominator


def solution(mesh):
    return jax.shard_map(
        shards,
        mesh=mesh,
        in_specs=(
            P(("parts", "pair"), None),
            P("parts"),
            P(("parts", "pair"), None),
            P(("parts", "pair"), None, None, None),
            P(("parts", "pair"), None),
            P(("parts", "pair"), None),
            P(("parts", "pair")),
            P("parts"),
        ),
        out_specs=P(("parts", "pair"), None),
        check_vma=False,
    )
```

profile of v0, /device:TPU:0, one launch (start us, length us, event | category | flops | bytes accessed | tf_op | source)
XLA Modules:
  0.0 96.8 jit_solution(1514602441448543067)
XLA Ops:
  0.0 0.7 copy.39
  1.6 0.7 iota_compare_fusion.1
  2.6 0.7 gather_fusion.1
  3.3 0.7 fusion.7
  4.0 7.4 %all-to-all-start = ((bf16[1,16,8,128]{3,2,0,1:T(8,128)(2,1)}), bf16[1,16,8,128]{3,2,0,1:T(8,128)(2,1)S(1)}, u32[]{:S(2)}, u32[]{:S(2)}) async-start(bf16[1,16,8,128]{3,2,0,1:T(8,128)(2,1)} %fusion.7), calls=%async_computation | async-start | bytes 65536 | tf_op jit(solution)/shard_map/all_to_all | solution.py:50
  12.1 0.8 broadcast_subtract_fusion
  12.9 0.8 gather_fusion.2
  13.7 21.8 %all-gather = bf16[16,1,16]{2,1,0:T(2,128)(2,1)S(1)} all-gather(bf16[1,1,16]{2,1,0:T(2,128)(2,1)} %bitcast.101), channel_id=1, replica_groups=mesh['parts'=2,'pair'=16] {'pair'}, dimensions={0}, use_global_device_ids=true | all-gather | bytes 544 | tf_op jit(solution)/shard_map/all_gather | solution.py:27
  35.8 4.1 %collective-permute-start.1 = (bf16[16,8,128]{2,0,1:T(8,128)(2,1)S(1)}, bf16[16,8,128]{2,0,1:T(8,128)(2,1)S(1)}, u32[]{:S(2)}, u32[]{:S(2)}) collective-permute-start(bf16[16,8,128]{2,0,1:T(8,128)(2,1)S(1)} %bitcast.98), channel_id=1, source_target_pairs={{1,0},{2,1},{3,2},{4,3},{5,4},{6,5},{7,6},{8,7},{9,8},{10,9},{11,1... | collective-permute-start | bytes 98312 | tf_op jit(solution)/shard_map/ppermute | solution.py:19
  40.7 3.5 %all-to-all-start.2 = ((f32[8,16,1,128]{3,0,2,1:T(8,128)}), f32[8,16,1,128]{3,0,2,1:T(8,128)S(1)}, u32[]{:S(2)}, u32[]{:S(2)}) async-start(f32[8,16,1,128]{3,0,2,1:T(8,128)} %copy.44), calls=%async_computation.2 | async-start | bytes 131072 | tf_op jit(solution)/shard_map/all_to_all | solution.py:81
  44.3 38.3 %while.10 = (s32[]{:T(128)}, f32[8,16,128]{2,0,1:T(8,128)}, s32[8,16]{1,0:T(8,128)}, bf16[16,24,128]{2,0,1:T(8,128)(2,1)S(1)}, bf16[8,16,128,128]{3,2,1,0:T(8,128)(2,1)}, /*index=5*/s32[]{:T(128)}, s32[]{:T(128)}) while((s32[]{:T(128)}, f32[8,16,128]{2,0,1:T(8,128)}, s32[8,16]{1,0:T(8,128)}, bf16[16,24,128]{2,0,1:T(8,128)(2,1)S(1)}, ...), condition=%wide.region_2.3_spmd, body=%wide.region_1.2_spmd.sunk | while | flops 8422546 | bytes 1798589 | solution.py:62
  46.3 1.1 %constant_dynamic-slice_fusion.3 = bf16[1,16,128,128]{3,2,1,0:T(8,128)(2,1)S(1)} fusion(bf16[8,16,128,128]{3,2,1,0:T(8,128)(2,1)} %get-tuple-element.102, s32[]{:T(128)} %get-tuple-element.91), kind=kLoop, calls=%fused_computation.14.clone.1 | loop fusion | bytes 1048580 | tf_op jit(solution)/shard_map/while/body/jit(dynamic_index_in_dim)/dynamic_slice | solution.py:62
  47.6 1.5 %dynamic_update_slice.5 = f32[8,16,128]{2,0,1:T(8,128)} dynamic-update-slice(f32[8,16,128]{2,0,1:T(8,128)} %get-tuple-element.92, f32[1,16,128]{2,0,1:T(1,128)S(1)} %bitcast.94, s32[]{:T(128)} %get-tuple-element.91, s32[]{:T(128)} %constant.47.clone.1..sunk, s32[]{:T(128)} %constant.47.clone.1..sunk) | dynamic-update-slice | bytes 16388 | tf_op jit(solution)/shard_map/while/body/jit(dynamic_update_index_in_dim)/dynamic_update_slice | solution.py:62
  50.4 0.7 compare_and_fusion.4
  51.1 1.1 %constant_dynamic-slice_fusion.3 = bf16[1,16,128,128]{3,2,1,0:T(8,128)(2,1)S(1)} fusion(bf16[8,16,128,128]{3,2,1,0:T(8,128)(2,1)} %get-tuple-element.102, s32[]{:T(128)} %get-tuple-element.91), kind=kLoop, calls=%fused_computation.14.clone.1 | loop fusion | bytes 1048580 | tf_op jit(solution)/shard_map/while/body/jit(dynamic_index_in_dim)/dynamic_slice | solution.py:62
  52.4 1.5 %dynamic_update_slice.5 = f32[8,16,128]{2,0,1:T(8,128)} dynamic-update-slice(f32[8,16,128]{2,0,1:T(8,128)} %get-tuple-element.92, f32[1,16,128]{2,0,1:T(1,128)S(1)} %bitcast.94, s32[]{:T(128)} %get-tuple-element.91, s32[]{:T(128)} %constant.47.clone.1..sunk, s32[]{:T(128)} %constant.47.clone.1..sunk) | dynamic-update-slice | bytes 16388 | tf_op jit(solution)/shard_map/while/body/jit(dynamic_update_index_in_dim)/dynamic_update_slice | solution.py:62
  55.8 1.1 %constant_dynamic-slice_fusion.3 = bf16[1,16,128,128]{3,2,1,0:T(8,128)(2,1)S(1)} fusion(bf16[8,16,128,128]{3,2,1,0:T(8,128)(2,1)} %get-tuple-element.102, s32[]{:T(128)} %get-tuple-element.91), kind=kLoop, calls=%fused_computation.14.clone.1 | loop fusion | bytes 1048580 | tf_op jit(solution)/shard_map/while/body/jit(dynamic_index_in_dim)/dynamic_slice | solution.py:62
  57.2 1.5 %dynamic_update_slice.5 = f32[8,16,128]{2,0,1:T(8,128)} dynamic-update-slice(f32[8,16,128]{2,0,1:T(8,128)} %get-tuple-element.92, f32[1,16,128]{2,0,1:T(1,128)S(1)} %bitcast.94, s32[]{:T(128)} %get-tuple-element.91, s32[]{:T(128)} %constant.47.clone.1..sunk, s32[]{:T(128)} %constant.47.clone.1..sunk) | dynamic-update-slice | bytes 16388 | tf_op jit(solution)/shard_map/while/body/jit(dynamic_update_index_in_dim)/dynamic_update_slice | solution.py:62
  59.9 0.7 compare_and_fusion.4
  60.6 1.1 %constant_dynamic-slice_fusion.3 = bf16[1,16,128,128]{3,2,1,0:T(8,128)(2,1)S(1)} fusion(bf16[8,16,128,128]{3,2,1,0:T(8,128)(2,1)} %get-tuple-element.102, s32[]{:T(128)} %get-tuple-element.91), kind=kLoop, calls=%fused_computation.14.clone.1 | loop fusion | bytes 1048580 | tf_op jit(solution)/shard_map/while/body/jit(dynamic_index_in_dim)/dynamic_slice | solution.py:62
  61.9 1.5 %dynamic_update_slice.5 = f32[8,16,128]{2,0,1:T(8,128)} dynamic-update-slice(f32[8,16,128]{2,0,1:T(8,128)} %get-tuple-element.92, f32[1,16,128]{2,0,1:T(1,128)S(1)} %bitcast.94, s32[]{:T(128)} %get-tuple-element.91, s32[]{:T(128)} %constant.47.clone.1..sunk, s32[]{:T(128)} %constant.47.clone.1..sunk) | dynamic-update-slice | bytes 16388 | tf_op jit(solution)/shard_map/while/body/jit(dynamic_update_index_in_dim)/dynamic_update_slice | solution.py:62
  65.4 1.1 %constant_dynamic-slice_fusion.3 = bf16[1,16,128,128]{3,2,1,0:T(8,128)(2,1)S(1)} fusion(bf16[8,16,128,128]{3,2,1,0:T(8,128)(2,1)} %get-tuple-element.102, s32[]{:T(128)} %get-tuple-element.91), kind=kLoop, calls=%fused_computation.14.clone.1 | loop fusion | bytes 1048580 | tf_op jit(solution)/shard_map/while/body/jit(dynamic_index_in_dim)/dynamic_slice | solution.py:62
  66.7 1.5 %dynamic_update_slice.5 = f32[8,16,128]{2,0,1:T(8,128)} dynamic-update-slice(f32[8,16,128]{2,0,1:T(8,128)} %get-tuple-element.92, f32[1,16,128]{2,0,1:T(1,128)S(1)} %bitcast.94, s32[]{:T(128)} %get-tuple-element.91, s32[]{:T(128)} %constant.47.clone.1..sunk, s32[]{:T(128)} %constant.47.clone.1..sunk) | dynamic-update-slice | bytes 16388 | tf_op jit(solution)/shard_map/while/body/jit(dynamic_update_index_in_dim)/dynamic_update_slice | solution.py:62
  70.2 1.1 %constant_dynamic-slice_fusion.3 = bf16[1,16,128,128]{3,2,1,0:T(8,128)(2,1)S(1)} fusion(bf16[8,16,128,128]{3,2,1,0:T(8,128)(2,1)} %get-tuple-element.102, s32[]{:T(128)} %get-tuple-element.91), kind=kLoop, calls=%fused_computation.14.clone.1 | loop fusion | bytes 1048580 | tf_op jit(solution)/shard_map/while/body/jit(dynamic_index_in_dim)/dynamic_slice | solution.py:62
  71.5 1.5 %dynamic_update_slice.5 = f32[8,16,128]{2,0,1:T(8,128)} dynamic-update-slice(f32[8,16,128]{2,0,1:T(8,128)} %get-tuple-element.92, f32[1,16,128]{2,0,1:T(1,128)S(1)} %bitcast.94, s32[]{:T(128)} %get-tuple-element.91, s32[]{:T(128)} %constant.47.clone.1..sunk, s32[]{:T(128)} %constant.47.clone.1..sunk) | dynamic-update-slice | bytes 16388 | tf_op jit(solution)/shard_map/while/body/jit(dynamic_update_index_in_dim)/dynamic_update_slice | solution.py:62
  74.3 0.7 compare_and_fusion.4
  75.0 1.1 %constant_dynamic-slice_fusion.3 = bf16[1,16,128,128]{3,2,1,0:T(8,128)(2,1)S(1)} fusion(bf16[8,16,128,128]{3,2,1,0:T(8,128)(2,1)} %get-tuple-element.102, s32[]{:T(128)} %get-tuple-element.91), kind=kLoop, calls=%fused_computation.14.clone.1 | loop fusion | bytes 1048580 | tf_op jit(solution)/shard_map/while/body/jit(dynamic_index_in_dim)/dynamic_slice | solution.py:62
  76.3 1.5 %dynamic_update_slice.5 = f32[8,16,128]{2,0,1:T(8,128)} dynamic-update-slice(f32[8,16,128]{2,0,1:T(8,128)} %get-tuple-element.92, f32[1,16,128]{2,0,1:T(1,128)S(1)} %bitcast.94, s32[]{:T(128)} %get-tuple-element.91, s32[]{:T(128)} %constant.47.clone.1..sunk, s32[]{:T(128)} %constant.47.clone.1..sunk) | dynamic-update-slice | bytes 16388 | tf_op jit(solution)/shard_map/while/body/jit(dynamic_update_index_in_dim)/dynamic_update_slice | solution.py:62
  79.8 1.1 %constant_dynamic-slice_fusion.3 = bf16[1,16,128,128]{3,2,1,0:T(8,128)(2,1)S(1)} fusion(bf16[8,16,128,128]{3,2,1,0:T(8,128)(2,1)} %get-tuple-element.102, s32[]{:T(128)} %get-tuple-element.91), kind=kLoop, calls=%fused_computation.14.clone.1 | loop fusion | bytes 1048580 | tf_op jit(solution)/shard_map/while/body/jit(dynamic_index_in_dim)/dynamic_slice | solution.py:62
  81.1 1.5 %dynamic_update_slice.5 = f32[8,16,128]{2,0,1:T(8,128)} dynamic-update-slice(f32[8,16,128]{2,0,1:T(8,128)} %get-tuple-element.92, f32[1,16,128]{2,0,1:T(1,128)S(1)} %bitcast.94, s32[]{:T(128)} %get-tuple-element.91, s32[]{:T(128)} %constant.47.clone.1..sunk, s32[]{:T(128)} %constant.47.clone.1..sunk) | dynamic-update-slice | bytes 16388 | tf_op jit(solution)/shard_map/while/body/jit(dynamic_update_index_in_dim)/dynamic_update_slice | solution.py:62
  82.6 6.0 %all-to-all-start.1 = ((f32[8,16,1,128]{3,0,2,1:T(8,128)}), f32[8,16,1,128]{3,0,2,1:T(8,128)S(1)}, u32[]{:S(2)}, u32[]{:S(2)}) async-start(f32[8,16,1,128]{3,0,2,1:T(8,128)} %bitcast.14), calls=%async_computation.1 | async-start | bytes 131072 | tf_op jit(solution)/shard_map/all_to_all | solution.py:74
  89.2 6.2 %all-to-all-done.1 = f32[8,16,1,128]{3,0,2,1:T(8,128)S(1)} async-done(((f32[8,16,1,128]{3,0,2,1:T(8,128)}), f32[8,16,1,128]{3,0,2,1:T(8,128)S(1)}, u32[]{:S(2)}, u32[]{:S(2)}) %all-to-all-start.1) | async-done | bytes 65568 | tf_op jit(solution)/shard_map/all_to_all | solution.py:74
  (70 shorter events, 19.9 us)
Async XLA Ops:
  0.0 2.5 %copy-start = (bf16[1,8192]{1,0:T(2,128)(2,1)S(1)}, bf16[1,8192]{1,0:T(2,128)(2,1)}, u32[]{:S(2)}) copy-start(bf16[1,8192]{1,0:T(2,128)(2,1)} %param.12) | copy-start | bytes 49156
  4.0 31.4 %all-to-all-start = ((bf16[1,16,8,128]{3,2,0,1:T(8,128)(2,1)}), bf16[1,16,8,128]{3,2,0,1:T(8,128)(2,1)S(1)}, u32[]{:S(2)}, u32[]{:S(2)}) async-start(bf16[1,16,8,128]{3,2,0,1:T(8,128)(2,1)} %fusion.7), calls=%async_computation | async-start | bytes 65536 | tf_op jit(solution)/shard_map/all_to_all | solution.py:50
  35.5 8.8 %collective-permute-start = (bf16[16,8,128]{2,0,1:T(8,128)(2,1)S(1)}, bf16[16,8,128]{2,0,1:T(8,128)(2,1)S(1)}, u32[]{:S(2)}, u32[]{:S(2)}) collective-permute-start(bf16[16,8,128]{2,0,1:T(8,128)(2,1)S(1)} %bitcast.97), channel_id=1, source_target_pairs={{0,1},{1,2},{2,3},{3,4},{4,5},{5,6},{6,7},{7,8},{8,9},{9,10},{10,1... | collective-permute-start | bytes 98312 | tf_op jit(solution)/shard_map/ppermute | solution.py:16
  35.8 8.4 %collective-permute-start.1 = (bf16[16,8,128]{2,0,1:T(8,128)(2,1)S(1)}, bf16[16,8,128]{2,0,1:T(8,128)(2,1)S(1)}, u32[]{:S(2)}, u32[]{:S(2)}) collective-permute-start(bf16[16,8,128]{2,0,1:T(8,128)(2,1)S(1)} %bitcast.98), channel_id=1, source_target_pairs={{1,0},{2,1},{3,2},{4,3},{5,4},{6,5},{7,6},{8,7},{9,8},{10,9},{11,1... | collective-permute-start | bytes 98312 | tf_op jit(solution)/shard_map/ppermute | solution.py:19
  40.7 41.9 %all-to-all-start.2 = ((f32[8,16,1,128]{3,0,2,1:T(8,128)}), f32[8,16,1,128]{3,0,2,1:T(8,128)S(1)}, u32[]{:S(2)}, u32[]{:S(2)}) async-start(f32[8,16,1,128]{3,0,2,1:T(8,128)} %copy.44), calls=%async_computation.2 | async-start | bytes 131072 | tf_op jit(solution)/shard_map/all_to_all | solution.py:81
  44.3 51.9 %copy-start.1 = (bf16[1,8192]{1,0:T(2,128)(2,1)S(1)}, bf16[1,8192]{1,0:T(2,128)(2,1)}, u32[]{:S(2)}) copy-start(bf16[1,8192]{1,0:T(2,128)(2,1)} %param.17) | copy-start | bytes 49156
  82.6 12.9 %all-to-all-start.1 = ((f32[8,16,1,128]{3,0,2,1:T(8,128)}), f32[8,16,1,128]{3,0,2,1:T(8,128)S(1)}, u32[]{:S(2)}, u32[]{:S(2)}) async-start(f32[8,16,1,128]{3,0,2,1:T(8,128)} %bitcast.14), calls=%async_computation.1 | async-start | bytes 131072 | tf_op jit(solution)/shard_map/all_to_all | solution.py:74
where the time goes:
time: 98.6 us; the launch traced here: 96.8 us
  local copies, waits for them, and re-layouts  29.4 us (30%)
  blocking collectives  21.8 us (22%)
  starting transfers between devices  21.3 us (22%)
  other arithmetic  15.3 us (16%)
  waiting for transfers between devices  6.26 us (6%)
  matrix products  1.96 us (2%)
    all_gather x1, blocking collectives, hole_product(): lax.all_gather(hole_ints, 'pair', axis=0, tiled=True)  21.8 us
    dynamic_update_slice x8, local copies, waits for them, and re-layouts, shards(): ladder = lax.map(ladder_slot, (screen, ladder_ints))  12 us
    dynamic_slice x8, local copies, waits for them, and re-layouts, shards(): ladder = lax.map(ladder_slot, (screen, ladder_ints))  8.61 us
    all_to_all x1, starting transfers between devices, shards(): lax.all_to_all(outgoing, 'pair', split_axis=1, concat_axis=0, tiled=True)  7.36 us
    all_to_all x1, waiting for transfers between devices, shards(): lax.all_to_all(ladder.reshape(CAP, pair_count, rows_dev, TILE), 'pair', s...  6.24 us
    all_to_all x1, starting transfers between devices, shards(): lax.all_to_all(ladder.reshape(CAP, pair_count, rows_dev, TILE), 'pair', s...  5.97 us
    and x8, other arithmetic, ladder_slot(): jnp.take(extended, chosen, axis=1).reshape(total_rows, coupling * TILE)  5.62 us
    select_n x8, other arithmetic, ladder_slot(): jnp.take(extended, chosen, axis=1).reshape(total_rows, coupling * TILE)  5.55 us
  transfers between devices with their start and end apart: 5, of which 1 were waited for; matrix products, arithmetic and copies ran while one was open for 43% of the time, Pallas kernels for 0%

commit v1 on v0

v1 whole, which is shorter than its diff:
```python
import functools

import jax
import jax.numpy as jnp
from jax import lax
from jax.experimental import pallas as pl
from jax.experimental.pallas import tpu as pltpu
from jax.sharding import PartitionSpec as P

TILE = 128
CAP = 8
MSG = 32
F32 = jnp.float32
BF16 = jnp.bfloat16


def each(count, body):
    if count <= 64:
        for i in range(count):
            body(i)
    else:
        def step(i, carry):
            body(i)
            return carry

        lax.fori_loop(0, count, step, 0)


def kernel(
    n,
    nt,
    nq,
    counts,
    screen,
    occ,
    amp_hbm,
    hole_hbm,
    ladder_hbm,
    direct_hbm,
    virt_hbm,
    out,
    amp_v,
    hole_v,
    ladder_v,
    direct_v,
    virt_v,
    tiles,
    direct_t,
    onehot,
    onehot_t,
    owned,
    send1,
    recv1,
    recv1_f,
    ext,
    coupled,
    send2,
    recv2,
    in_sem,
    ladder_sem,
    send1_sem,
    recv1_sem,
    send2_sem,
    recv2_sem,
):
    me = lax.axis_index("pair")
    cols = onehot.shape[1]

    copy_amp = pltpu.make_async_copy(amp_hbm, amp_v, in_sem.at[0])
    copy_hole = pltpu.make_async_copy(hole_hbm, hole_v, in_sem.at[1])
    copy_direct = pltpu.make_async_copy(direct_hbm, direct_v, in_sem.at[2])
    copy_virt = pltpu.make_async_copy(virt_hbm, virt_v, in_sem.at[3])
    copy_amp.start()
    copy_hole.start()

    barrier = pltpu.get_barrier_semaphore()

    def greet(t):
        pl.semaphore_signal(
            barrier, inc=1, device_id={"pair": lax.rem(me + 1 + t, n)}
        )

    each(n - 1, greet)

    ladder_copies = [
        pltpu.make_async_copy(ladder_hbm.at[s], ladder_v.at[s], ladder_sem.at[s])
        for s in range(CAP)
    ]
    for copy in ladder_copies:
        copy.start()
    copy_direct.start()
    copy_virt.start()

    lane = lax.broadcasted_iota(jnp.int32, (CAP, cols), 1)
    slot = lax.broadcasted_iota(jnp.int32, (CAP, cols), 0)

    def mark(e, offset):
        count = counts[e]
        hit = jnp.logical_and(lane == slot + offset, slot < count)
        row = e * CAP if isinstance(e, int) else pl.multiple_of(e * CAP, CAP)
        onehot[pl.ds(row, CAP), :] = jnp.where(hit, 1.0, 0.0).astype(F32)
        return offset + count

    if n <= 64:
        offset = jnp.int32(0)
        for e in range(n):
            offset = mark(e, offset)
    else:
        lax.fori_loop(0, n, mark, jnp.int32(0))

    copy_amp.wait()
    copy_hole.wait()
    tiles[pl.ds(nt, cols - nt), :] = jnp.zeros((cols - nt, TILE), F32)

    def lay(source, target):
        def body(t):
            at = t * TILE if isinstance(t, int) else pl.multiple_of(t * TILE, TILE)
            target[pl.ds(t, 1), :] = source[:, pl.ds(at, TILE)].astype(F32)

        each(nt, body)

    lay(amp_v, tiles)
    owned[...] = jnp.dot(
        onehot[...].astype(BF16), tiles[...].astype(BF16), preferred_element_type=F32
    )
    hole_row = jnp.concatenate(
        [hole_v[...].astype(F32), jnp.zeros((1, TILE - n), F32)], axis=1
    ) if n < TILE else hole_v[...].astype(F32)
    first = lax.broadcasted_iota(jnp.int32, (CAP, TILE), 0) == 0
    hole_block = jnp.where(first, jnp.broadcast_to(hole_row, (CAP, TILE)), 0.0)

    def compose(d):
        def block(e):
            row = e * CAP if isinstance(e, int) else pl.multiple_of(e * CAP, CAP)
            return owned[pl.ds(row, CAP), :]

        if isinstance(d, int):
            low, high = (d - 1) % n, (d + 1) % n
        else:
            low, high = lax.rem(d + n - 1, n), lax.rem(d + 1, n)
        send1[d] = jnp.concatenate(
            [block(low), block(d), block(high), hole_block], axis=0
        ).astype(BF16)

    each(n, compose)

    pl.semaphore_wait(barrier, n - 1)

    def to_owner(t):
        d = lax.rem(me + 1 + t, n)
        pltpu.make_async_remote_copy(
            src_ref=send1.at[d],
            dst_ref=recv1.at[me],
            send_sem=send1_sem,
            recv_sem=recv1_sem,
            device_id={"pair": d},
        ).start()

    each(n - 1, to_owner)
    recv1[me] = send1[me]

    onehot_t[...] = onehot[...].T.astype(BF16)
    copy_direct.wait()
    copy_virt.wait()
    lay(direct_v, direct_t)

    def everything(send, recv, send_sem, recv_sem):
        return pltpu.make_async_remote_copy(
            src_ref=send.at[pl.ds(0, n - 1)],
            dst_ref=recv.at[pl.ds(0, n - 1)],
            send_sem=send_sem,
            recv_sem=recv_sem,
            device_id={"pair": lax.rem(me + 1, n)},
        )

    everything(send1, recv1, send1_sem, recv1_sem).wait_recv()

    recv1_f[...] = recv1[...].astype(F32).reshape(n * MSG, TILE)
    for j in range(3 * CAP):
        ext[j] = recv1_f[pl.ds(j, n, stride=MSG), :].astype(BF16)
    holes = recv1_f[pl.ds(3 * CAP, n, stride=MSG), :][:, :n].astype(BF16)

    for s in range(CAP):
        ladder_copies[s].wait()
        picked = jnp.concatenate([ext[screen[s, k]] for k in range(nq)], axis=1)
        ladder = jnp.dot(picked, ladder_v[s], preferred_element_type=F32)
        hole = jnp.dot(holes, ext[CAP + s], preferred_element_type=F32)
        coupled[pl.ds(s * n, n), :] = ladder + hole

    def to_row(t):
        d = lax.rem(me + 1 + t, n)
        pltpu.make_async_remote_copy(
            src_ref=send2.at[d],
            dst_ref=recv2.at[me],
            send_sem=send2_sem,
            recv_sem=recv2_sem,
            device_id={"pair": d},
        ).start()

    def split(i):
        send2[i] = coupled[pl.ds(i, CAP, stride=n), :]

    each(n, split)
    each(n - 1, to_row)
    recv2[me] = send2[me]
    everything(send2, recv2, send2_sem, recv2_sem).wait_recv()

    home = recv2[...].reshape(n * CAP, TILE).astype(BF16)
    sums = jnp.dot(onehot_t[...], home, preferred_element_type=F32)[:nt]
    out[...] = (direct_t[...] + sums) / (virt_v[...] - occ[0])
    everything(send1, recv1, send1_sem, recv1_sem).wait_send()
    everything(send2, recv2, send2_sem, recv2_sem).wait_send()


def shards(
    amplitudes, tile_counts, screen, ladder_ints, hole_ints, direct, occ_energy, virt_energy
):
    n = lax.axis_size("pair")
    nt = amplitudes.shape[1] // TILE
    nq = screen.shape[1]
    cols = -(-nt // TILE) * TILE
    if cols == nt:
        cols += TILE
    smem = pl.BlockSpec(memory_space=pltpu.SMEM)
    hbm = pl.BlockSpec(memory_space=pl.ANY)
    updated = pl.pallas_call(
        functools.partial(kernel, n, nt, nq),
        out_shape=jax.ShapeDtypeStruct((nt, TILE), F32),
        in_specs=[smem, smem, smem, hbm, hbm, hbm, hbm, hbm],
        out_specs=pl.BlockSpec(memory_space=pltpu.VMEM),
        scratch_shapes=[
            pltpu.VMEM((1, nt * TILE), BF16),
            pltpu.VMEM((1, n), BF16),
            pltpu.VMEM((CAP, nq * TILE, TILE), BF16),
            pltpu.VMEM((1, nt * TILE), BF16),
            pltpu.VMEM((nt, TILE), F32),
            pltpu.VMEM((cols, TILE), F32),
            pltpu.VMEM((nt, TILE), F32),
            pltpu.VMEM((n * CAP, cols), F32),
            pltpu.VMEM((cols, n * CAP), BF16),
            pltpu.VMEM((n * CAP, TILE), F32),
            pltpu.VMEM((n, MSG, TILE), BF16),
            pltpu.VMEM((n, MSG, TILE), BF16),
            pltpu.VMEM((n * MSG, TILE), F32),
            pltpu.VMEM((3 * CAP, n, TILE), BF16),
            pltpu.VMEM((CAP * n, TILE), F32),
            pltpu.VMEM((n, CAP, TILE), F32),
            pltpu.VMEM((n, CAP, TILE), F32),
            pltpu.SemaphoreType.DMA((4,)),
            pltpu.SemaphoreType.DMA((CAP,)),
            pltpu.SemaphoreType.DMA,
            pltpu.SemaphoreType.DMA,
            pltpu.SemaphoreType.DMA,
            pltpu.SemaphoreType.DMA,
        ],
        compiler_params=pltpu.CompilerParams(
            collective_id=0, has_side_effects=True, vmem_limit_bytes=48 * 1024 * 1024
        ),
        cost_estimate=pl.CostEstimate(
            flops=2 * CAP * nq * TILE * TILE * n,
            bytes_accessed=CAP * nq * TILE * TILE * 2,
            transcendentals=0,
        ),
    )(
        tile_counts,
        screen,
        occ_energy,
        amplitudes,
        hole_ints,
        ladder_ints.reshape(CAP, nq * TILE, TILE),
        direct,
        virt_energy.reshape(nt, TILE),
    )
    return updated.reshape(1, nt * TILE)


def solution(mesh):
    return jax.shard_map(
        shards,
        mesh=mesh,
        in_specs=(
            P(("parts", "pair"), None),
            P("parts"),
            P(("parts", "pair"), None),
            P(("parts", "pair"), None, None, None),
            P(("parts", "pair"), None),
            P(("parts", "pair"), None),
            P(("parts", "pair")),
            P("parts"),
        ),
        out_specs=P(("parts", "pair"), None),
        check_vma=False,
    )
```

time: 98.6 us -> 26.1 us (0.26); the launches traced: 96.8 us -> 25.7 us
  local copies, waits for them, and re-layouts: 29.4 us -> 7.07 us
  blocking collectives: 21.8 us -> 0 us
  starting transfers between devices: 21.3 us -> 0 us
  Pallas kernels: 0 us -> 18 us
  other arithmetic: 15.3 us -> 0 us
  waiting for transfers between devices: 6.26 us -> 0 us
  matrix products: 1.96 us -> 0 us
    all_gather x1 -> x0, blocking collectives: 21.8 us -> none  [hole_product(): lax.all_gather(hole_ints, 'pair', axis=0, tiled=True)]
    pallas_call x0 -> x1, Pallas kernels: none -> 18 us  [shards(): pl.pallas_call(functools.partial(kernel, n, nt, nq), out_shape=jax.ShapeD...]
    all_to_all x3 -> x0, starting transfers between devices: 16.8 us -> none  [the longest x1 7.36 us: shards(): lax.all_to_all(outgoing, 'pair', split_axis=1, concat_axis=0, tiled=True)]
    dynamic_update_slice x8 -> x0, local copies, waits for them, and re-layouts: 12 us -> none  [shards(): ladder = lax.map(ladder_slot, (screen, ladder_ints))]
    dynamic_slice x8 -> x0, local copies, waits for them, and re-layouts: 8.61 us -> none  [shards(): ladder = lax.map(ladder_slot, (screen, ladder_ints))]
    gather x12 -> x0, local copies, waits for them, and re-layouts: 7.26 us -> none  [the longest x8 4.58 us: ladder_slot(): jnp.take(extended, chosen, axis=1).reshape(total_rows, coupling * TILE)]
    unnamed x4 -> x15, local copies, waits for them, and re-layouts: 0.01 us -> 7.07 us
    select_n x11 -> x0, other arithmetic: 6.28 us -> none  [the longest x8 5.55 us: ladder_slot(): jnp.take(extended, chosen, axis=1).reshape(total_rows, coupling * TILE)]
  transfers between devices with their start and end apart: 5 -> 0, of which waited for: 1 -> 0; matrix products, arithmetic and copies ran while one was open for 43% -> 0% of each run, Pallas kernels for 0% -> 0%
where the time goes in v1:
time: 26.1 us; the launch traced here: 25.7 us
  Pallas kernels  18 us (69%)
  local copies, waits for them, and re-layouts  7.07 us (27%)
  between operations  0.67 us (3%)
    pallas_call x1, Pallas kernels, shards(): pl.pallas_call(functools.partial(kernel, n, nt, nq), out_shape=jax.ShapeD...  18 us
    unnamed x15, local copies, waits for them, and re-layouts  7.07 us

profile of v1, /device:TPU:0, one launch (start us, length us, event | category | flops | bytes accessed | tf_op | source)
XLA Modules:
  0.0 25.7 jit_solution(10658369717840766871)
XLA Ops:
  0.7 0.0 copy-start
  0.7 2.2 %copy-done = bf16[8,16,128,128]{3,2,1,0:T(8,128)(2,1)S(1)} copy-done((bf16[8,16,128,128]{3,2,1,0:T(8,128)(2,1)S(1)}, bf16[8,16,128,128]{3,2,1,0:T(8,128)(2,1)}, u32[]{:S(2)}) %copy-start) | copy-done | bytes 4194328
  2.8 0.0 copy-start.1
  2.8 0.8 %copy-done.1 = bf16[1,8192]{1,0:T(2,128)(2,1)S(1)} copy-done((bf16[1,8192]{1,0:T(2,128)(2,1)S(1)}, bf16[1,8192]{1,0:T(2,128)(2,1)}, u32[]{:S(2)}) %copy-start.1) | copy-done | bytes 16408
  3.6 0.0 copy-start.2
  3.6 0.8 %copy-done.2 = bf16[1,8192]{1,0:T(2,128)(2,1)S(1)} copy-done((bf16[1,8192]{1,0:T(2,128)(2,1)S(1)}, bf16[1,8192]{1,0:T(2,128)(2,1)}, u32[]{:S(2)}) %copy-start.2) | copy-done | bytes 16408
  4.4 0.0 copy-start.3
  4.4 0.8 %copy-done.3 = f32[8192]{0:T(1024)S(1)} copy-done((f32[8192]{0:T(1024)S(1)}, f32[8192]{0:T(1024)}, u32[]{:S(2)}) %copy-start.3) | copy-done | bytes 32792
  5.1 0.0 copy-start.4
  5.1 0.7 %copy-done.4 = s32[8,16]{1,0:T(8,128)S(1)} copy-done((s32[8,16]{1,0:T(8,128)S(1)}, s32[8,16]{1,0:T(8,128)}, u32[]{:S(2)}) %copy-start.4) | copy-done | bytes 536
  5.8 0.0 copy-start.5
  5.8 0.7 %copy-done.5 = s32[16]{0:T(128)S(1)} copy-done((s32[16]{0:T(128)S(1)}, s32[16]{0:T(128)}, u32[]{:S(2)}) %copy-start.5) | copy-done | bytes 88
  6.5 0.0 copy-start.6
  6.5 0.7 %copy-done.6 = bf16[1,16]{1,0:T(2,128)(2,1)S(1)} copy-done((bf16[1,16]{1,0:T(2,128)(2,1)S(1)}, bf16[1,16]{1,0:T(2,128)(2,1)}, u32[]{:S(2)}) %copy-start.6) | copy-done | bytes 56
  7.1 18.0 %shard_map.82 = f32[64,128]{1,0:T(8,128)S(1)} custom-call(s32[16]{0:T(128)S(1)} %copy-done.5, s32[8,16]{1,0:T(8,128)S(1)} %copy-done.4, f32[1]{0:T(128)S(6)} %copy.10.occ, bf16[1,8192]{1,0:T(2,128)(2,1)S(1)} %copy-done.1, bf16[1,16]{1,0:T(2,128)(2,1)S(1)} %copy-done.6, bf16[8,2048,128]{2,1,0:T(8,128)(2,1)S(1)} %bitcast.3, bf16[1,8192]{1,0:T(2,128)(2,1)S(1)} %copy-done.2, ...), custom_call_target="tpu_custom_call" | custom-call | flops 67108864 | bytes 4194304 | tf_op jit(solution)/shard_map/pallas_call | solution.py:226
  25.1 0.6 %copy.11 = f32[1,8192]{1,0:T(1,128)} copy(f32[1,8192]{1,0:T(1,128)S(1)} %bitcast.4) | data formatting | bytes 65536
Async XLA Ops:
  0.7 2.2 %copy-start = (bf16[8,16,128,128]{3,2,1,0:T(8,128)(2,1)S(1)}, bf16[8,16,128,128]{3,2,1,0:T(8,128)(2,1)}, u32[]{:S(2)}) copy-start(bf16[8,16,128,128]{3,2,1,0:T(8,128)(2,1)} %param.11) | copy-start | bytes 12582916
  2.8 0.8 %copy-start.1 = (bf16[1,8192]{1,0:T(2,128)(2,1)S(1)}, bf16[1,8192]{1,0:T(2,128)(2,1)}, u32[]{:S(2)}) copy-start(bf16[1,8192]{1,0:T(2,128)(2,1)} %amp_hbm.1) | copy-start | bytes 49156
  3.6 0.8 %copy-start.2 = (bf16[1,8192]{1,0:T(2,128)(2,1)S(1)}, bf16[1,8192]{1,0:T(2,128)(2,1)}, u32[]{:S(2)}) copy-start(bf16[1,8192]{1,0:T(2,128)(2,1)} %direct_hbm.1) | copy-start | bytes 49156
  4.4 0.8 %copy-start.3 = (f32[8192]{0:T(1024)S(1)}, f32[8192]{0:T(1024)}, u32[]{:S(2)}) copy-start(f32[8192]{0:T(1024)} %param.15) | copy-start | bytes 98308
  5.1 0.7 %copy-start.4 = (s32[8,16]{1,0:T(8,128)S(1)}, s32[8,16]{1,0:T(8,128)}, u32[]{:S(2)}) copy-start(s32[8,16]{1,0:T(8,128)} %screen.1) | copy-start | bytes 1540
  5.8 0.7 %copy-start.5 = (s32[16]{0:T(128)S(1)}, s32[16]{0:T(128)}, u32[]{:S(2)}) copy-start(s32[16]{0:T(128)} %counts.1) | copy-start | bytes 196
  6.5 0.7 %copy-start.6 = (bf16[1,16]{1,0:T(2,128)(2,1)S(1)}, bf16[1,16]{1,0:T(2,128)(2,1)}, u32[]{:S(2)}) copy-start(bf16[1,16]{1,0:T(2,128)(2,1)} %hole_hbm.1) | copy-start | bytes 100

commit v2 on v1

--- a/solution.py
+++ b/solution.py
@@ -30,15 +30,18 @@
     n,
     nt,
     nq,
-    counts,
-    screen,
-    occ,
+    counts_hbm,
+    screen_hbm,
+    occ_hbm,
     amp_hbm,
     hole_hbm,
     ladder_hbm,
     direct_hbm,
     virt_hbm,
     out,
+    counts,
+    screen,
+    occ,
     amp_v,
     hole_v,
     ladder_v,
@@ -70,6 +73,10 @@
     copy_hole = pltpu.make_async_copy(hole_hbm, hole_v, in_sem.at[1])
     copy_direct = pltpu.make_async_copy(direct_hbm, direct_v, in_sem.at[2])
     copy_virt = pltpu.make_async_copy(virt_hbm, virt_v, in_sem.at[3])
+    copy_counts = pltpu.make_async_copy(counts_hbm, counts, in_sem.at[4])
+    copy_screen = pltpu.make_async_copy(screen_hbm, screen, in_sem.at[5])
+    copy_occ = pltpu.make_async_copy(occ_hbm, occ, in_sem.at[6])
+    copy_counts.start()
     copy_amp.start()
     copy_hole.start()
 
@@ -88,8 +95,10 @@
     ]
     for copy in ladder_copies:
         copy.start()
+    copy_screen.start()
     copy_direct.start()
     copy_virt.start()
+    copy_occ.start()
 
     lane = lax.broadcasted_iota(jnp.int32, (CAP, cols), 1)
     slot = lax.broadcasted_iota(jnp.int32, (CAP, cols), 0)
@@ -101,6 +110,7 @@
         onehot[pl.ds(row, CAP), :] = jnp.where(hit, 1.0, 0.0).astype(F32)
         return offset + count
 
+    copy_counts.wait()
     if n <= 64:
         offset = jnp.int32(0)
         for e in range(n):
@@ -162,6 +172,8 @@
     onehot_t[...] = onehot[...].T.astype(BF16)
     copy_direct.wait()
     copy_virt.wait()
+    copy_screen.wait()
+    copy_occ.wait()
     lay(direct_v, direct_t)
 
     def everything(send, recv, send_sem, recv_sem):
@@ -221,14 +233,16 @@
     cols = -(-nt // TILE) * TILE
     if cols == nt:
         cols += TILE
-    smem = pl.BlockSpec(memory_space=pltpu.SMEM)
-    hbm = pl.BlockSpec(memory_space=pl.ANY)
+    hbm = pl.BlockSpec(memory_space=pltpu.HBM)
     updated = pl.pallas_call(
         functools.partial(kernel, n, nt, nq),
         out_shape=jax.ShapeDtypeStruct((nt, TILE), F32),
-        in_specs=[smem, smem, smem, hbm, hbm, hbm, hbm, hbm],
+        in_specs=[hbm] * 8,
         out_specs=pl.BlockSpec(memory_space=pltpu.VMEM),
         scratch_shapes=[
+            pltpu.SMEM((n,), jnp.int32),
+            pltpu.SMEM((CAP, nq), jnp.int32),
+            pltpu.SMEM((1,), F32),
             pltpu.VMEM((1, nt * TILE), BF16),
             pltpu.VMEM((1, n), BF16),
             pltpu.VMEM((CAP, nq * TILE, TILE), BF16),
@@ -246,7 +260,7 @@
             pltpu.VMEM((CAP * n, TILE), F32),
             pltpu.VMEM((n, CAP, TILE), F32),
             pltpu.VMEM((n, CAP, TILE), F32),
-            pltpu.SemaphoreType.DMA((4,)),
+            pltpu.SemaphoreType.DMA((7,)),
             pltpu.SemaphoreType.DMA((CAP,)),
             pltpu.SemaphoreType.DMA,
             pltpu.SemaphoreType.DMA,
@@ -254,7 +268,7 @@
             pltpu.SemaphoreType.DMA,
         ],
         compiler_params=pltpu.CompilerParams(
-            collective_id=0, has_side_effects=True, vmem_limit_bytes=48 * 1024 * 1024
+            collective_id=0, has_side_effects=True, vmem_limit_bytes=62 * 1024 * 1024
         ),
         cost_estimate=pl.CostEstimate(
             flops=2 * CAP * nq * TILE * TILE * n,

time: 26.1 us -> 20.2 us (0.77)
  local copies, waits for them, and re-layouts: 7.07 us -> 1.38 us
    unnamed x15 -> x1, local copies, waits for them, and re-layouts: 7.07 us -> 1.38 us
where the time goes in v2:
time: 20.2 us; the launch traced here: 20 us
  Pallas kernels  18 us (89%)
  local copies, waits for them, and re-layouts  1.38 us (7%)
  between operations  0.66 us (3%)
    pallas_call x1, Pallas kernels, shards(): pl.pallas_call(functools.partial(kernel, n, nt, nq), out_shape=jax.ShapeD...  18 us
    unnamed x1, local copies, waits for them, and re-layouts  1.38 us

profile of v2, /device:TPU:0, one launch (start us, length us, event | category | flops | bytes accessed | tf_op | source)
XLA Modules:
  0.0 20.0 jit_solution(4232026350916832191)
XLA Ops:
  0.7 18.0 %shard_map.82 = f32[64,128]{1,0:T(8,128)} custom-call(s32[16]{0:T(128)} %counts_hbm.1, s32[8,16]{1,0:T(8,128)} %screen_hbm.1, f32[1]{0:T(128)S(6)} %copy.10.occ_hbm, bf16[1,8192]{1,0:T(2,128)(2,1)} %amp_hbm.1, bf16[1,16]{1,0:T(2,128)(2,1)} %hole_hbm.1, bf16[8,2048,128]{2,1,0:T(8,128)(2,1)} %bitcast.3, bf16[1,8192]{1,0:T(2,128)(2,1)} %direct_hbm.1, ...), custom_call_target="tpu_custom_call" | custom-call | flops 67108864 | bytes 4194304 | tf_op jit(solution)/shard_map/pallas_call | solution.py:237
  18.6 1.4 %copy.11 = f32[1,8192]{1,0:T(1,128)} copy(f32[1,8192]{1,0:T(1,128)} %bitcast.4) | data formatting | bytes 65536

commit v3 on v2

--- a/solution.py
+++ b/solution.py
@@ -9,6 +9,7 @@
 
 TILE = 128
 CAP = 8
+GROUP = 4
 MSG = 32
 F32 = jnp.float32
 BF16 = jnp.bfloat16
@@ -24,6 +25,17 @@
             return carry
 
         lax.fori_loop(0, count, step, 0)
+
+
+def far_first(n):
+    if n % GROUP or n > 64:
+        return None
+    groups = n // GROUP
+    ends = []
+    for far in range(1, groups // 2 + 1):
+        ends.append([groups - far] if 2 * far == groups else [groups - far, far])
+    steps = [(far, near) for pair in ends for near in range(GROUP) for far in pair]
+    return steps + [(0, near) for near in range(1, GROUP)]
 
 
 def kernel(
@@ -68,6 +80,15 @@
 ):
     me = lax.axis_index("pair")
     cols = onehot.shape[1]
+    steps = far_first(n)
+
+    def to_peers(body):
+        if steps is None:
+            each(n - 1, lambda t: body(lax.rem(me + 1 + t, n)))
+        else:
+            for far, near in steps:
+                group = lax.rem(me // GROUP + far, n // GROUP)
+                body(group * GROUP + lax.rem(me + near, GROUP))
 
     copy_amp = pltpu.make_async_copy(amp_hbm, amp_v, in_sem.at[0])
     copy_hole = pltpu.make_async_copy(hole_hbm, hole_v, in_sem.at[1])
@@ -141,23 +162,17 @@
 
     def compose(d):
         def block(e):
-            row = e * CAP if isinstance(e, int) else pl.multiple_of(e * CAP, CAP)
-            return owned[pl.ds(row, CAP), :]
-
-        if isinstance(d, int):
-            low, high = (d - 1) % n, (d + 1) % n
-        else:
-            low, high = lax.rem(d + n - 1, n), lax.rem(d + 1, n)
+            return owned[pl.ds(pl.multiple_of(e * CAP, CAP), CAP), :]
+
+        low, high = lax.rem(d + n - 1, n), lax.rem(d + 1, n)
         send1[d] = jnp.concatenate(
             [block(low), block(d), block(high), hole_block], axis=0
         ).astype(BF16)
 
-    each(n, compose)
-
     pl.semaphore_wait(barrier, n - 1)
 
-    def to_owner(t):
-        d = lax.rem(me + 1 + t, n)
+    def to_owner(d):
+        compose(d)
         pltpu.make_async_remote_copy(
             src_ref=send1.at[d],
             dst_ref=recv1.at[me],
@@ -166,7 +181,8 @@
             device_id={"pair": d},
         ).start()
 
-    each(n - 1, to_owner)
+    to_peers(to_owner)
+    compose(me)
     recv1[me] = send1[me]
 
     onehot_t[...] = onehot[...].T.astype(BF16)
@@ -199,8 +215,11 @@
         hole = jnp.dot(holes, ext[CAP + s], preferred_element_type=F32)
         coupled[pl.ds(s * n, n), :] = ladder + hole
 
-    def to_row(t):
-        d = lax.rem(me + 1 + t, n)
+    def split(i):
+        send2[i] = coupled[pl.ds(i, CAP, stride=n), :]
+
+    def to_row(d):
+        split(d)
         pltpu.make_async_remote_copy(
             src_ref=send2.at[d],
             dst_ref=recv2.at[me],
@@ -209,11 +228,8 @@
             device_id={"pair": d},
         ).start()
 
-    def split(i):
-        send2[i] = coupled[pl.ds(i, CAP, stride=n), :]
-
-    each(n, split)
-    each(n - 1, to_row)
+    to_peers(to_row)
+    split(me)
     recv2[me] = send2[me]
     everything(send2, recv2, send2_sem, recv2_sem).wait_recv()
 

time: 20.2 us -> 20.1 us (level)
  no operation moved by 1% of the time
where the time goes in v3:
time: 20.1 us; the launch traced here: 19.9 us
  Pallas kernels  17.9 us (89%)
  local copies, waits for them, and re-layouts  1.38 us (7%)
  between operations  0.66 us (3%)
    pallas_call x1, Pallas kernels, shards(): pl.pallas_call(functools.partial(kernel, n, nt, nq), out_shape=jax.ShapeD...  17.9 us
    unnamed x1, local copies, waits for them, and re-layouts  1.38 us

profile of v3, /device:TPU:0, one launch (start us, length us, event | category | flops | bytes accessed | tf_op | source)
XLA Modules:
  0.0 19.9 jit_solution(9176517458209330489)
XLA Ops:
  0.7 17.9 %shard_map.82 = f32[64,128]{1,0:T(8,128)} custom-call(s32[16]{0:T(128)} %counts_hbm.1, s32[8,16]{1,0:T(8,128)} %screen_hbm.1, f32[1]{0:T(128)S(6)} %copy.10.occ_hbm, bf16[1,8192]{1,0:T(2,128)(2,1)} %amp_hbm.1, bf16[1,16]{1,0:T(2,128)(2,1)} %hole_hbm.1, bf16[8,2048,128]{2,1,0:T(8,128)(2,1)} %bitcast.3, bf16[1,8192]{1,0:T(2,128)(2,1)} %direct_hbm.1, ...), custom_call_target="tpu_custom_call" | custom-call | flops 67108864 | bytes 4194304 | tf_op jit(solution)/shard_map/pallas_call | solution.py:253
  18.5 1.4 %copy.11 = f32[1,8192]{1,0:T(1,128)} copy(f32[1,8192]{1,0:T(1,128)} %bitcast.4) | data formatting | bytes 65536

commit v4 on v3

--- a/solution.py
+++ b/solution.py
@@ -284,7 +284,7 @@
             pltpu.SemaphoreType.DMA,
         ],
         compiler_params=pltpu.CompilerParams(
-            collective_id=0, has_side_effects=True, vmem_limit_bytes=62 * 1024 * 1024
+            collective_id=0, has_side_effects=True, vmem_limit_bytes=48 * 1024 * 1024
         ),
         cost_estimate=pl.CostEstimate(
             flops=2 * CAP * nq * TILE * TILE * n,
@@ -292,14 +292,21 @@
             transcendentals=0,
         ),
     )(
-        tile_counts,
-        screen,
-        occ_energy,
-        amplitudes,
-        hole_ints,
-        ladder_ints.reshape(CAP, nq * TILE, TILE),
-        direct,
-        virt_energy.reshape(nt, TILE),
+        *[
+            operand
+            if operand.size == 1
+            else pltpu.with_memory_space_constraint(operand, pltpu.HBM)
+            for operand in (
+                tile_counts,
+                screen,
+                occ_energy,
+                amplitudes,
+                hole_ints,
+                ladder_ints.reshape(CAP, nq * TILE, TILE),
+                direct,
+                virt_energy.reshape(nt, TILE),
+            )
+        ]
     )
     return updated.reshape(1, nt * TILE)
 

time: 20.1 us -> 18.7 us (0.930)
  local copies, waits for them, and re-layouts: 1.38 us -> 0.62 us
  Pallas kernels: 17.9 us -> 17.3 us
    unnamed x1, local copies, waits for them, and re-layouts: 1.38 us -> 0.62 us
    pallas_call x1, Pallas kernels: 17.9 us -> 17.3 us  [shards(): pl.pallas_call(functools.partial(kernel, n, nt, nq), out_shape=jax.ShapeD...]
where the time goes in v4:
time: 18.7 us; the launch traced here: 18.6 us
  Pallas kernels  17.3 us (93%)
  between operations  0.66 us (4%)
  local copies, waits for them, and re-layouts  0.62 us (3%)
    pallas_call x1, Pallas kernels, shards(): pl.pallas_call(functools.partial(kernel, n, nt, nq), out_shape=jax.ShapeD...  17.3 us
    unnamed x1, local copies, waits for them, and re-layouts  0.62 us

profile of v4, /device:TPU:0, one launch (start us, length us, event | category | flops | bytes accessed | tf_op | source)
XLA Modules:
  0.0 18.6 jit_solution(15735250653328552678)
XLA Ops:
  0.7 17.3 %shard_map.82 = f32[64,128]{1,0:T(8,128)S(1)} custom-call(s32[16]{0:T(128)} %counts_hbm.1, s32[8,16]{1,0:T(8,128)} %screen_hbm.1, f32[1]{0:T(128)S(6)} %copy.10.occ_hbm, bf16[1,8192]{1,0:T(2,128)(2,1)} %amp_hbm.1, bf16[1,16]{1,0:T(2,128)(2,1)} %hole_hbm.1, bf16[8,2048,128]{2,1,0:T(8,128)(2,1)} %bitcast.4, bf16[1,8192]{1,0:T(2,128)(2,1)} %direct_hbm.1, ...), custom_call_target="tpu_custom_call" | custom-call | flops 67108864 | bytes 4194304 | tf_op jit(solution)/shard_map/pallas_call | solution.py:253
  17.9 0.6 %copy.11 = f32[1,8192]{1,0:T(1,128)} copy(f32[1,8192]{1,0:T(1,128)S(1)} %bitcast.3) | data formatting | bytes 65536

commit v5 on v4

--- a/solution.py
+++ b/solution.py
@@ -103,12 +103,10 @@
 
     barrier = pltpu.get_barrier_semaphore()
 
-    def greet(t):
-        pl.semaphore_signal(
-            barrier, inc=1, device_id={"pair": lax.rem(me + 1 + t, n)}
-        )
-
-    each(n - 1, greet)
+    def greet(d):
+        pl.semaphore_signal(barrier, inc=1, device_id={"pair": d})
+
+    to_peers(greet)
 
     ladder_copies = [
         pltpu.make_async_copy(ladder_hbm.at[s], ladder_v.at[s], ladder_sem.at[s])

time: 18.7 us -> 18.8 us (level)
  no operation moved by 1% of the time
where the time goes in v5:
time: 18.8 us; the launch traced here: 18.6 us
  Pallas kernels  17.3 us (92%)
  between operations  0.66 us (4%)
  local copies, waits for them, and re-layouts  0.62 us (3%)
    pallas_call x1, Pallas kernels, shards(): pl.pallas_call(functools.partial(kernel, n, nt, nq), out_shape=jax.ShapeD...  17.3 us
    unnamed x1, local copies, waits for them, and re-layouts  0.62 us

profile of v5, /device:TPU:0, one launch (start us, length us, event | category | flops | bytes accessed | tf_op | source)
XLA Modules:
  0.0 18.6 jit_solution(12182623606841767847)
XLA Ops:
  0.7 17.3 %shard_map.82 = f32[64,128]{1,0:T(8,128)S(1)} custom-call(s32[16]{0:T(128)} %counts_hbm.1, s32[8,16]{1,0:T(8,128)} %screen_hbm.1, f32[1]{0:T(128)S(6)} %copy.10.occ_hbm, bf16[1,8192]{1,0:T(2,128)(2,1)} %amp_hbm.1, bf16[1,16]{1,0:T(2,128)(2,1)} %hole_hbm.1, bf16[8,2048,128]{2,1,0:T(8,128)(2,1)} %bitcast.4, bf16[1,8192]{1,0:T(2,128)(2,1)} %direct_hbm.1, ...), custom_call_target="tpu_custom_call" | custom-call | flops 67108864 | bytes 4194304 | tf_op jit(solution)/shard_map/pallas_call | solution.py:251
  18.0 0.6 %copy.11 = f32[1,8192]{1,0:T(1,128)} copy(f32[1,8192]{1,0:T(1,128)S(1)} %bitcast.3) | data formatting | bytes 65536

commit v6 on v5

--- a/solution.py
+++ b/solution.py
@@ -112,12 +112,6 @@
         pltpu.make_async_copy(ladder_hbm.at[s], ladder_v.at[s], ladder_sem.at[s])
         for s in range(CAP)
     ]
-    for copy in ladder_copies:
-        copy.start()
-    copy_screen.start()
-    copy_direct.start()
-    copy_virt.start()
-    copy_occ.start()
 
     lane = lax.broadcasted_iota(jnp.int32, (CAP, cols), 1)
     slot = lax.broadcasted_iota(jnp.int32, (CAP, cols), 0)
@@ -180,6 +174,12 @@
         ).start()
 
     to_peers(to_owner)
+    for copy in ladder_copies:
+        copy.start()
+    copy_screen.start()
+    copy_direct.start()
+    copy_virt.start()
+    copy_occ.start()
     compose(me)
     recv1[me] = send1[me]
 

time: 18.8 us -> 18.8 us (level)
  no operation moved by 1% of the time
where the time goes in v6:
time: 18.8 us; the launch traced here: 18.6 us
  Pallas kernels  17.3 us (92%)
  between operations  0.66 us (4%)
  local copies, waits for them, and re-layouts  0.62 us (3%)
    pallas_call x1, Pallas kernels, shards(): pl.pallas_call(functools.partial(kernel, n, nt, nq), out_shape=jax.ShapeD...  17.3 us
    unnamed x1, local copies, waits for them, and re-layouts  0.62 us

profile of v6, /device:TPU:0, one launch (start us, length us, event | category | flops | bytes accessed | tf_op | source)
XLA Modules:
  0.0 18.6 jit_solution(2258105123785714480)
XLA Ops:
  0.7 17.3 %shard_map.82 = f32[64,128]{1,0:T(8,128)S(1)} custom-call(s32[16]{0:T(128)} %counts_hbm.1, s32[8,16]{1,0:T(8,128)} %screen_hbm.1, f32[1]{0:T(128)S(6)} %copy.10.occ_hbm, bf16[1,8192]{1,0:T(2,128)(2,1)} %amp_hbm.1, bf16[1,16]{1,0:T(2,128)(2,1)} %hole_hbm.1, bf16[8,2048,128]{2,1,0:T(8,128)(2,1)} %bitcast.4, bf16[1,8192]{1,0:T(2,128)(2,1)} %direct_hbm.1, ...), custom_call_target="tpu_custom_call" | custom-call | flops 67108864 | bytes 4194304 | tf_op jit(solution)/shard_map/pallas_call | solution.py:251
  18.0 0.6 %copy.11 = f32[1,8192]{1,0:T(1,128)} copy(f32[1,8192]{1,0:T(1,128)S(1)} %bitcast.3) | data formatting | bytes 65536
